TPU v7x, 32 devices: a whole 2x2x4 slice. The times are simulated.
32 devices in a mesh: rve: 2 (over x), branch: 16 (over z, y, core).
Axes of the slice: x: 2, y: 2, z: 4, core: 2. Of those that a mesh axis runs over, the one named last changes fastest.
Arguments:
- loads: bfloat16 [2048, 32, 192], P(('rve', 'branch')), parts along dimension 0, may hold values from -6 to 6
- basis: bfloat16 [2048, 32, 192], P(('rve', 'branch')), parts along dimension 0, may hold values from -0.4375 to 0.4375
- transfer: bfloat16 [2048, 32, 32], P(('rve', 'branch')), parts along dimension 0, may hold values from -0.375 to 0.375
- near_blocks: bfloat16 [3072, 192, 192], P(('rve', 'branch')), parts along dimension 0, may hold values from -0.4375 to 0.4375
- near_src: int32 [3072], P(('rve', 'branch')), parts along dimension 0, may hold values from -1 to 1023, as said below
- near_tgt: int32 [3072], P(('rve', 'branch')), parts along dimension 0, may hold values from 0 to 1023, as said below
- far_blocks: bfloat16 [8192, 32, 32], P(('rve', 'branch')), parts along dimension 0, may hold values from -1 to 1
- far_src: int32 [8192], P(('rve', 'branch')), parts along dimension 0, may hold values from -1 to 1023, as said below
- far_tgt: int32 [8192], P(('rve', 'branch')), parts along dimension 0, may hold values from 0 to 1023, as said below
- coarse_blocks: bfloat16 [2048, 32, 32], P(('rve', 'branch')), parts along dimension 0, may hold values from -1 to 1
- coarse_src: int32 [2048], P(('rve', 'branch')), parts along dimension 0, may hold values from -1 to 127, as said below
- coarse_tgt: int32 [2048], P(('rve', 'branch')), parts along dimension 0, may hold values from 0 to 127, as said below
Outputs:
- response: bfloat16 [2048, 32, 192], P(('rve', 'branch')), parts along dimension 0
There are 2 independent parts, one for each index of `rve`. A program takes and returns all parts, laid end to end along the dimension named above; each array names one. Nothing has to cross between parts.
Inputs may be any that keep to these rules, and one draw needn't show every extreme that they name: `near_src`: entries of one device's block of 96 name -1 or a leaf at most 64 leaves before the device's first leaf or after its last one. `near_tgt`: entries of one device's block of 96 name leaves of that device. `far_src`: in one device's block of 256 entries at most 32 name leaves of any one device, and exactly 32 name leaves of some device; at least half of the entries are not -1. `far_tgt`: entries of one device's block of 256 name leaves of that device. `coarse_src`: in one device's block of 64 entries at most 8 name parents held by any one device (parents q with q // 8 equal), and exactly 8 for some device; at least half are not -1. `coarse_tgt`: entries of one device's block of 64 name parents of that device's leaves.
All inputs are finite; a program needn't handle non-finite values.
Results may differ from a plain program's by a relative error of at most 0.005.
Values may be sent and summed in bfloat16 or wider, within the bound.
A program may use at most 128 MiB of HBM per device.

v0:
```python
import jax
import jax.numpy as jnp
from jax import lax
from jax.sharding import PartitionSpec as P


def with_halo(cells, sides, width):
    for axis, dim in sides:
        count = lax.axis_size(axis)
        ends = count - 1
        head = lax.slice_in_dim(cells, 0, width, axis=dim)
        tail = lax.slice_in_dim(cells, cells.shape[dim] - width, cells.shape[dim], axis=dim)
        cells = jnp.concatenate(
            [
                lax.ppermute(tail, axis, [(i, (i + 1) % count) for i in range(ends)]),
                cells,
                lax.ppermute(head, axis, [((i + 1) % count, i) for i in range(ends)]),
            ],
            axis=dim,
        )
    return cells


def scatter_rows(terms, targets, count):
    selector = (targets[None, :] == jnp.arange(count, dtype=jnp.int32)[:, None]).astype(jnp.float32)
    flat_terms = terms.reshape(terms.shape[0], -1)
    summed = jnp.dot(
        selector, flat_terms, precision=lax.Precision.HIGHEST, preferred_element_type=jnp.float32
    )
    return summed.reshape((count,) + terms.shape[1:])


def shards(
    loads,
    basis,
    transfer,
    near_blocks,
    near_src,
    near_tgt,
    far_blocks,
    far_src,
    far_tgt,
    coarse_blocks,
    coarse_src,
    coarse_tgt,
):
    leaf_count, cases, width = loads.shape
    rank = basis.shape[1]
    parent_count = leaf_count // 8
    position = lax.axis_index("branch")
    leaf_base = position * leaf_count
    parent_base = position * parent_count
    leaf_coef = jnp.einsum("lcp,lrp->lcr", loads, basis, preferred_element_type=jnp.float32).astype(
        jnp.bfloat16
    )
    lifted = jnp.einsum("lcr,lrs->lcs", leaf_coef, transfer, preferred_element_type=jnp.float32)
    parent_coef = lifted.reshape(parent_count, 8, cases, rank).sum(axis=1).astype(jnp.bfloat16)
    leaf_flat = leaf_coef.reshape(leaf_count, cases * rank)
    parent_flat = parent_coef.reshape(parent_count, cases * rank)
    far_count = far_src.shape[0]
    coarse_count = coarse_src.shape[0]
    every_leaf, every_parent = (
        lax.all_gather(leaf_flat, "branch", axis=0, tiled=True),
        lax.all_gather(parent_flat, "branch", axis=0, tiled=True),
    )
    far_live = far_src >= 0
    coarse_live = coarse_src >= 0
    far_rows = jnp.take(every_leaf, jnp.clip(far_src, 0, every_leaf.shape[0] - 1), axis=0)
    coarse_rows = jnp.take(every_parent, jnp.clip(coarse_src, 0, every_parent.shape[0] - 1), axis=0)
    far_terms = jnp.einsum(
        "ncr,nrs->ncs",
        far_rows.reshape(far_count, cases, rank),
        far_blocks,
        preferred_element_type=jnp.float32,
    )
    far_terms = far_terms * far_live.astype(jnp.float32)[:, None, None]
    far_field = scatter_rows(far_terms, far_tgt - leaf_base, leaf_count)
    coarse_terms = jnp.einsum(
        "ncr,nrs->ncs",
        coarse_rows.reshape(coarse_count, cases, rank),
        coarse_blocks,
        preferred_element_type=jnp.float32,
    )
    coarse_terms = coarse_terms * coarse_live.astype(jnp.float32)[:, None, None]
    coarse_field = scatter_rows(coarse_terms, coarse_tgt - parent_base, parent_count).astype(
        jnp.bfloat16
    )
    downward = jnp.einsum(
        "lcs,lrs->lcr",
        jnp.repeat(coarse_field, 8, axis=0),
        transfer,
        preferred_element_type=jnp.float32,
    )
    local_coef = (far_field + downward).astype(jnp.bfloat16)
    far_out = jnp.einsum("lcr,lrp->lcp", local_coef, basis, preferred_element_type=jnp.float32)
    widened = with_halo(loads, (("branch", 0),), leaf_count)
    near_live = near_src >= 0
    near_index = jnp.clip(near_src - leaf_base + leaf_count, 0, 3 * leaf_count - 1)
    near_rows = jnp.take(widened, near_index, axis=0)
    near_terms = jnp.einsum(
        "ncp,npq->ncq", near_rows, near_blocks, preferred_element_type=jnp.float32
    )
    near_terms = near_terms * near_live.astype(jnp.float32)[:, None, None]
    near_field = scatter_rows(near_terms, near_tgt - leaf_base, leaf_count)
    return (far_out + near_field).astype(jnp.bfloat16)


def solution(mesh):
    in_specs = (
        P(("rve", "branch"), None, None),
        P(("rve", "branch"), None, None),
        P(("rve", "branch"), None, None),
        P(("rve", "branch"), None, None),
        P(("rve", "branch")),
        P(("rve", "branch")),
        P(("rve", "branch"), None, None),
        P(("rve", "branch")),
        P(("rve", "branch")),
        P(("rve", "branch"), None, None),
        P(("rve", "branch")),
        P(("rve", "branch")),
    )
    out_specs = P(("rve", "branch"), None, None)
    return jax.shard_map(shards, mesh=mesh, in_specs=in_specs, out_specs=out_specs, check_vma=False)
```

profile of v0, /device:TPU:0, one launch (start us, length us, event | category | flops | bytes accessed | tf_op | source)
XLA Modules:
  0.0 122.5 jit_solution(4579065620839501413)
XLA Ops:
  6.5 0.0 copy-start
  6.5 0.0 copy-start.5
  6.5 0.0 all-gather.2.cloned.1.call-start
  6.5 1.4 %collective-permute-start.1 = (bf16[64,32,192]{2,1,0:T(8,128)(2,1)}, bf16[64,32,192]{2,1,0:T(8,128)(2,1)}, u32[]{:S(2)}, u32[]{:S(2)}) collective-permute-start(bf16[64,32,192]{2,1,0:T(8,128)(2,1)} %param.12), channel_id=1, source_target_pairs={{1,0},{2,1},{3,2},{4,3},{5,4},{6,5},{7,6},{8,7},{9,8},{10,9},{11,1... | collective-permute-start | bytes 2359304 | tf_op jit(solution)/shard_map/ppermute | solution.py:17
  8.0 4.0 %collective-permute-start = (bf16[64,32,192]{2,1,0:T(8,128)(2,1)}, bf16[64,32,192]{2,1,0:T(8,128)(2,1)}, u32[]{:S(2)}, u32[]{:S(2)}) collective-permute-start(bf16[64,32,192]{2,1,0:T(8,128)(2,1)} %param.12), channel_id=1, source_target_pairs={{0,1},{1,2},{2,3},{3,4},{4,5},{5,6},{6,7},{7,8},{8,9},{9,10},{10,1... | collective-permute-start | bytes 2359304 | tf_op jit(solution)/shard_map/ppermute | solution.py:15
  12.0 0.0 copy-done
  12.0 1.6 %convolution_convert_fusion = bf16[64,32,32]{2,1,0:T(8,128)(2,1)S(1)} fusion(bf16[64,32,192]{2,1,0:T(8,128)(2,1)} %param.12, bf16[64,32,192]{2,1,0:T(8,128)(2,1)S(1)} %copy-done), kind=kOutput, calls=%fused_computation.13 | convolution fusion | flops 25231360 | bytes 1703936 | tf_op jit(solution)/shard_map/lcp,lrp->lcr/dot_general | solution.py:53
  13.6 0.0 copy-start.10
  13.7 0.6 copy.20
  14.2 0.8 copy.21
  15.0 0.0 all-gather.2.cloned.1.call-update
  15.0 0.0 copy-done.5
  15.1 0.9 copy.35
  15.9 0.0 copy-start.3
  16.0 0.0 copy-start.6
  16.0 0.4 bitcast_reduce_fusion
  16.4 0.1 convert_element_type.34
  16.5 0.0 copy-done.10
  16.5 0.2 copy-done.3
  16.8 32.3 %all_gather.7 = bf16[128,1024]{1,0:T(8,128)(2,1)S(1)} all-gather(bf16[8,1024]{1,0:T(8,128)(2,1)S(1)} %convert_element_type.34), channel_id=1, replica_groups=mesh['rve'=2,'branch'=16] {'branch'}, dimensions={0}, use_global_device_ids=true | all-gather | bytes 278528 | tf_op jit(solution)/shard_map/all_gather | solution.py:64
  49.1 0.7 gather_fusion.1
  49.8 0.2 copy.27
  50.0 0.8 copy.28
  50.8 0.0 copy-done.6
  50.8 0.0 copy-start.11
  50.8 0.0 copy-start.7
  50.8 0.0 copy-start.9
  50.8 0.8 copy.29
  51.6 0.3 convolution_multiply_fusion.2
  51.9 0.0 copy-start.12
  51.9 0.0 copy-start.8
  51.9 0.0 copy-start.4
  51.9 1.4 %copy.30 = f32[64,32,32]{0,2,1:T(8,128)} copy(f32[64,32,32]{2,1,0:T(8,128)S(1)} %convolution_multiply_fusion.2) | data formatting | bytes 524288 | tf_op jit(solution)/shard_map/mul | solution.py:84
  53.3 0.0 copy-done.11
  53.3 0.0 copy-done.7
  53.3 0.0 copy-done.9
  53.3 2.2 %convolution_convert_fusion.1 = bf16[8,32,32]{2,0,1:T(8,128)(2,1)S(1)} fusion(f32[64,32,32]{0,2,1:T(8,128)} %copy.30, s32[64]{0:T(128)S(1)} %broadcast_subtract_fusion.2), kind=kOutput, calls=%fused_computation.14 | convolution fusion | flops 6300160 | bytes 278784 | tf_op jit(solution)/shard_map/dot_general | solution.py:27
  55.5 4.8 %copy.24 = bf16[256,32,32]{2,1,0:T(8,128)(2,1)} copy(bf16[256,32,32]{0,2,1:T(8,128)(2,1)} %param.18) | data formatting | bytes 1048576 | tf_op args[6]
  60.3 0.0 copy-done.12
  60.3 0.0 copy-done.8
  60.4 0.0 collective-permute-done.1
  60.4 0.0 collective-permute-done
  60.4 0.0 copy-done.4
  60.4 3.2 %pad_maximum_fusion = bf16[192,32,192]{2,1,0:T(8,128)(2,1)} fusion(bf16[64,32,192]{2,1,0:T(8,128)(2,1)} %collective-permute-done.1, bf16[64,32,192]{2,1,0:T(8,128)(2,1)S(1)} %copy-done.4, bf16[64,32,192]{2,1,0:T(8,128)(2,1)} %collective-permute-done), kind=kLoop, calls=%fused_computation.3 | loop fusion | flops 2359296 | bytes 4718592 | tf_op jit(solution)/shard_map/concatenate | solution.py:13
  63.7 2.6 %gather_fusion.2 = bf16[96,32,192]{2,1,0:T(8,128)(2,1)S(1)} fusion(bf16[192,32,192]{2,1,0:T(8,128)(2,1)} %pad_maximum_fusion, s32[1024]{0:T(1024)S(1)} %pad_clamp_fusion), kind=kCustom, calls=%fused_computation.2 | custom fusion | bytes 2359680 | tf_op jit(solution)/shard_map/jit(_take)/gather | solution.py:99
  66.3 7.3 %convolution_multiply_fusion.1 = f32[96,32,192]{2,1,0:T(8,128)} fusion(bf16[96,192,192]{2,1,0:T(8,128)(2,1)} %param.15, f32[96]{0:T(128)S(1)} %get-tuple-element.12, bf16[96,32,192]{2,1,0:T(8,128)(2,1)S(1)} %gather_fusion.2, pred[96]{0:T(512)(128)(4,1)S(1)} %get-tuple-element.7), kind=kOutput, calls=%fused_computation.7 | convolution fusion | flops 227672064 | bytes 10617312 | tf_op jit(solution)/shard_map/ncp,npq->ncq/dot_general | solution.py:100
  73.6 3.1 %reshape.67 = f32[96,6144]{1,0:T(8,128)S(1)} reshape(f32[96,32,192]{2,1,0:T(8,128)} %convolution_multiply_fusion.1) | data formatting | bytes 4718592 | tf_op jit(solution)/shard_map/reshape | solution.py:26
  76.6 2.4 %copy.32 = f32[6144,96]{1,0:T(8,128)} copy(f32[6144,96]{0,1:T(8,128)S(1)} %bitcast.45) | data formatting | bytes 4718592 | tf_op jit(solution)/shard_map/dot_general | solution.py:27
  79.0 6.3 %fusion.12 = f32[64,32,192]{2,0,1:T(8,128)} fusion(f32[32,192,96]{2,1,0:T(8,128)} %bitcast.44, s32[96]{0:T(128)S(1)} %broadcast_subtract_fusion.1), kind=kOutput, calls=%fused_computation.27 | convolution fusion | flops 452990976 | bytes 3932544 | tf_op jit(solution)/shard_map/dot_general | solution.py:27
  85.3 0.0 all-gather.2.cloned.1.call-done
  85.3 3.4 %gather_fusion = bf16[256,1024]{1,0:T(8,128)(2,1)S(1)} fusion(bf16[1024,1024]{1,0:T(8,128)(2,1)} %all-gather.2.cloned.1.call-done, s32[1024]{0:T(1024)S(1)} %pad_clamp_fusion.2), kind=kCustom, calls=%fused_computation | custom fusion | bytes 1049600 | tf_op jit(solution)/shard_map/jit(_take)/gather | solution.py:68
  88.8 1.0 copy.22
  89.8 0.0 copy-start.1
  89.8 2.0 %broadcast_select_fusion = bf16[256,32,32]{0,2,1:T(8,128)(2,1)} fusion(bf16[256,32,32]{0,2,1:T(8,128)(2,1)} %bitcast.47, pred[256]{0:T(512)(128)(4,1)S(1)} %get-tuple-element.10), kind=kLoop, calls=%fused_computation.20 | loop fusion | flops 262144 | bytes 1048832 | tf_op jit(solution)/shard_map/jit(_take)/select_n | solution.py:68
  91.8 4.6 %copy.23 = bf16[256,32,32]{2,1,0:T(8,128)(2,1)} copy(bf16[256,32,32]{0,2,1:T(8,128)(2,1)} %broadcast_select_fusion) | data formatting | bytes 1048576 | tf_op jit(solution)/shard_map/jit(_take)/select_n | solution.py:68
  96.4 0.0 copy-done.1
  96.4 4.3 %convolution_multiply_fusion = f32[256,32,32]{2,1,0:T(8,128)} fusion(bf16[256,32,32]{2,1,0:T(8,128)(2,1)} %copy.23, bf16[256,32,32]{2,1,0:T(8,128)(2,1)S(1)} %copy-done.1, f32[256]{0:T(256)S(1)} %get-tuple-element.9), kind=kOutput, calls=%fused_computation.4 | convolution fusion | flops 17039360 | bytes 2098176 | tf_op jit(solution)/shard_map/ncr,nrs->ncs/dot_general | solution.py:70
  100.7 4.3 %copy.25 = f32[256,32,32]{0,2,1:T(8,128)} copy(f32[256,32,32]{2,1,0:T(8,128)} %convolution_multiply_fusion) | data formatting | bytes 2097152 | tf_op jit(solution)/shard_map/mul | solution.py:76
  105.0 0.0 copy-start.2
  105.0 2.8 %fusion.4 = f32[64,32,32]{0,2,1:T(8,128)} fusion(f32[256,32,32]{0,2,1:T(8,128)} %copy.25, s32[256]{0:T(256)S(1)} %broadcast_subtract_fusion), kind=kOutput, calls=%fused_computation.15 | convolution fusion | flops 201342976 | bytes 1311744 | tf_op jit(solution)/shard_map/dot_general | solution.py:27
  107.8 2.8 %copy.34 = f32[64,32,32]{2,1,0:T(8,128)} copy(f32[64,32,32]{0,2,1:T(8,128)} %fusion.4) | data formatting | bytes 524288 | tf_op jit(solution)/shard_map/dot_general | solution.py:27
  110.6 0.9 broadcast_in_dim.54
  111.5 0.0 copy-done.2
  111.5 4.1 %fusion = bf16[64,32,192]{2,1,0:T(8,128)(2,1)} fusion(f32[64,32,192]{2,0,1:T(8,128)S(1)} %copy-done.2, bf16[64,32,192]{2,1,0:T(8,128)(2,1)S(1)} %copy-done, f32[64,32,32]{2,1,0:T(8,128)} %copy.34, bf16[64,32,32]{2,1,0:T(8,128)(2,1)} %bitcast.46, bf16[64,32,32]{1,2,0:T(8,128)(2,1)} %copy-done.3), kind=kOutput, calls=%fused_computation.6 | convolution fusion | flops 30277632 | bytes 3670016 | tf_op jit(solution)/shard_map/lcr,lrp->lcp/dot_general | solution.py:95
  (12 shorter events, 0.1 us)
Async XLA Ops:
  6.5 5.5 %copy-start = (bf16[64,32,192]{2,1,0:T(8,128)(2,1)S(1)}, bf16[64,32,192]{2,1,0:T(8,128)(2,1)}, u32[]{:S(2)}) copy-start(bf16[64,32,192]{2,1,0:T(8,128)(2,1)} %param.13) | copy-start | bytes 2359300
  6.5 8.5 %copy-start.5 = (bf16[64,32,32]{0,2,1:T(8,128)(2,1)S(1)}, bf16[64,32,32]{0,2,1:T(8,128)(2,1)}, u32[]{:S(2)}) copy-start(bf16[64,32,32]{0,2,1:T(8,128)(2,1)} %param.14) | copy-start | bytes 393220
  6.5 78.8 %all-gather.2.cloned.1.call-start = ((), (), s32[]{:S(2)}) async-start(), calls=%async_computation | async-start | bytes 2228224 | tf_op jit(solution)/shard_map/all_gather | solution.py:63
  6.5 53.8 %collective-permute-start.1 = (bf16[64,32,192]{2,1,0:T(8,128)(2,1)}, bf16[64,32,192]{2,1,0:T(8,128)(2,1)}, u32[]{:S(2)}, u32[]{:S(2)}) collective-permute-start(bf16[64,32,192]{2,1,0:T(8,128)(2,1)} %param.12), channel_id=1, source_target_pairs={{1,0},{2,1},{3,2},{4,3},{5,4},{6,5},{7,6},{8,7},{9,8},{10,9},{11,1... | collective-permute-start | bytes 2359304 | tf_op jit(solution)/shard_map/ppermute | solution.py:17
  8.0 52.4 %collective-permute-start = (bf16[64,32,192]{2,1,0:T(8,128)(2,1)}, bf16[64,32,192]{2,1,0:T(8,128)(2,1)}, u32[]{:S(2)}, u32[]{:S(2)}) collective-permute-start(bf16[64,32,192]{2,1,0:T(8,128)(2,1)} %param.12), channel_id=1, source_target_pairs={{0,1},{1,2},{2,3},{3,4},{4,5},{5,6},{6,7},{7,8},{8,9},{9,10},{10,1... | collective-permute-start | bytes 2359304 | tf_op jit(solution)/shard_map/ppermute | solution.py:15
  13.6 2.9 %copy-start.10 = (s32[64]{0:T(128)S(1)}, s32[64]{0:T(128)}, u32[]{:S(2)}) copy-start(s32[64]{0:T(128)} %param.22) | copy-start | bytes 772
  15.9 0.8 copy-start.3
  16.0 34.8 %copy-start.6 = (bf16[64,32,32]{0,2,1:T(8,128)(2,1)S(1)}, bf16[64,32,32]{0,2,1:T(8,128)(2,1)}, u32[]{:S(2)}) copy-start(bf16[64,32,32]{0,2,1:T(8,128)(2,1)} %param.21) | copy-start | bytes 393220
  50.8 2.5 %copy-start.11 = (s32[64]{0:T(128)S(1)}, s32[64]{0:T(128)}, u32[]{:S(2)}) copy-start(s32[64]{0:T(128)} %param.23) | copy-start | bytes 772
  50.8 2.5 %copy-start.7 = (s32[256]{0:T(256)S(1)}, s32[256]{0:T(256)}, u32[]{:S(2)}) copy-start(s32[256]{0:T(256)} %param.19) | copy-start | bytes 3076
  50.8 2.5 %copy-start.9 = (s32[96]{0:T(128)S(1)}, s32[96]{0:T(128)}, u32[]{:S(2)}) copy-start(s32[96]{0:T(128)} %param.16) | copy-start | bytes 1156
  51.9 8.5 %copy-start.12 = (s32[96]{0:T(128)S(1)}, s32[96]{0:T(128)}, u32[]{:S(2)}) copy-start(s32[96]{0:T(128)} %param.17) | copy-start | bytes 1156
  51.9 8.5 %copy-start.8 = (s32[256]{0:T(256)S(1)}, s32[256]{0:T(256)}, u32[]{:S(2)}) copy-start(s32[256]{0:T(256)} %param.20) | copy-start | bytes 3076
  51.9 8.5 %copy-start.4 = (bf16[64,32,192]{2,1,0:T(8,128)(2,1)S(1)}, bf16[64,32,192]{2,1,0:T(8,128)(2,1)}, u32[]{:S(2)}) copy-start(bf16[64,32,192]{2,1,0:T(8,128)(2,1)} %param.12) | copy-start | bytes 2359300
  89.8 6.6 %copy-start.1 = (bf16[256,32,32]{2,1,0:T(8,128)(2,1)S(1)}, bf16[256,32,32]{2,1,0:T(8,128)(2,1)}, u32[]{:S(2)}) copy-start(bf16[256,32,32]{2,1,0:T(8,128)(2,1)} %copy.24) | copy-start | bytes 1572868
  105.0 6.5 %copy-start.2 = (f32[64,32,192]{2,0,1:T(8,128)S(1)}, f32[64,32,192]{2,0,1:T(8,128)}, u32[]{:S(2)}) copy-start(f32[64,32,192]{2,0,1:T(8,128)} %fusion.12) | copy-start | bytes 4718596
Sparse Core Ops, SparseCore 0:
  15.2 45.3 all-gather.1
where the time goes:
time: 124 us; the launch traced here: 123 us
  local copies, waits for them, and re-layouts  36.3 us (29%)
  blocking collectives  32.3 us (26%)
  matrix products  29.4 us (24%)
  between operations  13.7 us (11%)
  starting transfers between devices  5.44 us (4%)
  other arithmetic  5.39 us (4%)
    all_gather x1, blocking collectives, shards(): lax.all_gather(parent_flat, 'branch', axis=0, tiled=True)  32.3 us
    dot_general x3, matrix products, scatter_rows(): jnp.dot(selector, flat_terms, precision=lax.Precision.HIGHEST, preferred_...  11.3 us
    dot_general x1, matrix products, shards(): jnp.einsum('ncp,npq->ncq', near_rows, near_blocks, preferred_element_type...  7.29 us
    unnamed x29, local copies, waits for them, and re-layouts  6.71 us
    dot_general x2, local copies, waits for them, and re-layouts, scatter_rows(): jnp.dot(selector, flat_terms, precision=lax.Precision.HIGHEST, preferred_...  5.17 us
    select_n x1, local copies, waits for them, and re-layouts, shards(): jnp.take(every_leaf, jnp.clip(far_src, 0, every_leaf.shape[0] - 1), axis=0)  4.57 us
    gather x2, local copies, waits for them, and re-layouts, shards(): jnp.take(every_leaf, jnp.clip(far_src, 0, every_leaf.shape[0] - 1), axis=0)  4.42 us
    mul x1, local copies, waits for them, and re-layouts, shards(): far_terms = far_terms * far_live.astype(jnp.float32)[:, None, None]  4.34 us
  transfers between devices with their start and end apart: 3, of which 0 were waited for; matrix products, arithmetic and copies ran while one was open for 33% of the time, Pallas kernels for 0%

commit v1 on v0

v1 whole, which is shorter than its diff:
```python
import jax
import jax.numpy as jnp
from jax import lax
from jax.experimental import pallas as pl
from jax.experimental.pallas import tpu as pltpu
from jax.sharding import PartitionSpec as P

F32, BF16 = jnp.float32, jnp.bfloat16
VMEM = pl.BlockSpec(memory_space=pltpu.VMEM)
SMEM = pl.BlockSpec(memory_space=pltpu.SMEM)
PACK = 4
NT = (((1,), (1,)), ((), ()))


def div(x, n):
    return lax.shift_right_logical(x, n.bit_length() - 1) if n & (n - 1) == 0 else lax.div(x, n)


def dot(a, b):
    return jnp.dot(a, b, preferred_element_type=F32)


def dot_nt(a, b):
    return lax.dot_general(a, b, NT, preferred_element_type=F32)


def lane_slot(shape, rank):
    return div(lax.broadcasted_iota(jnp.int32, shape, 1), rank)


def upward(loads_ref, basis_ref, transfer_ref, out_ref):
    leaves, cases, width = loads_ref.shape
    rank = basis_ref.shape[1]
    groups = leaves // PACK
    slot = lane_slot((cases, PACK * rank), rank)
    per_parent = 8 // PACK
    parents = []
    total = None
    for g in range(groups):
        part = pl.ds(PACK * g, PACK)
        full = dot_nt(
            loads_ref[part].reshape(PACK * cases, width), basis_ref[part].reshape(PACK * rank, width)
        )
        packed = full[:cases]
        for k in range(1, PACK):
            packed = jnp.where(slot == k, full[k * cases : (k + 1) * cases], packed)
        packed = packed.astype(BF16)
        out_ref[g] = packed
        term = dot(packed, transfer_ref[part].reshape(PACK * rank, rank))
        total = term if g % per_parent == 0 else total + term
        if g % per_parent == per_parent - 1:
            parents.append(total)
    for h in range(len(parents) // PACK):
        out_ref[groups + h] = jnp.concatenate(parents[PACK * h : PACK * h + PACK], axis=1).astype(BF16)


def near(src_ref, tgt_ref, left_ref, own_ref, right_ref, blocks_ref, out_ref, wide):
    step = pl.program_id(0)
    leaves = own_ref.shape[0]
    base = lax.axis_index("branch") * leaves
    chunk = blocks_ref.shape[0]

    @pl.when(step == 0)
    def _():
        wide[pl.ds(0, leaves)] = left_ref[...]
        wide[pl.ds(leaves, leaves)] = own_ref[...]
        wide[pl.ds(2 * leaves, leaves)] = right_ref[...]
        wide[3 * leaves] = jnp.zeros(wide.shape[1:], BF16)
        out_ref[...] = jnp.zeros_like(out_ref)

    terms = []
    for i in range(chunk):
        s = src_ref[step * chunk + i]
        row = jnp.where(s < 0, 3 * leaves, jnp.clip(s - base + leaves, 0, 3 * leaves - 1))
        terms.append(dot(wide[row], blocks_ref[i]))
    for i in range(chunk):
        t = jnp.clip(tgt_ref[step * chunk + i] - base, 0, leaves - 1)
        out_ref[t] += terms[i]


def downward(
    fsrc_ref, ftgt_ref, csrc_ref, ctgt_ref, coef_ref, far_ref, coarse_ref, transfer_ref, basis_ref,
    near_ref, out_ref, facc, cacc
):
    leaves, rank, width = basis_ref.shape
    cases = out_ref.shape[1]
    parents = leaves // 8
    groups = leaves // PACK
    tiles = groups + parents // PACK
    position = lax.axis_index("branch")
    slot = lane_slot((cases, PACK * rank), rank)
    facc[...] = jnp.zeros_like(facc)
    cacc[...] = jnp.zeros_like(cacc)

    def couple(src_ref, block_ref, held, shift, j):
        s = src_ref[j]
        a = jnp.maximum(s, 0)
        dev = div(a, held)
        inner = a - dev * held
        tile = div(inner, PACK)
        k = jnp.where(s < 0, -1, inner - tile * PACK)
        lhs = coef_ref[dev * tiles + shift + tile]
        lhs = jnp.where(slot == k, lhs, jnp.zeros_like(lhs))
        return dot(lhs, jnp.concatenate([block_ref[j]] * PACK, axis=0))

    unroll = 16

    def far_step(i, carry):
        terms = [couple(fsrc_ref, far_ref, leaves, 0, i * unroll + u) for u in range(unroll)]
        for u in range(unroll):
            t = jnp.clip(ftgt_ref[i * unroll + u] - position * leaves, 0, leaves - 1)
            tile = div(t, PACK)
            facc[tile] += jnp.where(slot == t - tile * PACK, terms[u], 0.0)
        return carry

    def coarse_step(i, carry):
        terms = [couple(csrc_ref, coarse_ref, parents, groups, i * unroll + u) for u in range(unroll)]
        for u in range(unroll):
            t = jnp.clip(ctgt_ref[i * unroll + u] - position * parents, 0, parents - 1)
            cacc[t] += terms[u]
        return carry

    lax.fori_loop(0, csrc_ref.shape[0] // unroll, coarse_step, 0)
    lax.fori_loop(0, fsrc_ref.shape[0] // unroll, far_step, 0)
    for g in range(groups):
        part = pl.ds(PACK * g, PACK)
        coarse = cacc[g * PACK // 8][:, :rank].astype(BF16)
        down = dot_nt(coarse, transfer_ref[part].reshape(PACK * rank, rank))
        local = (facc[g] + down).astype(BF16)
        spread = jnp.concatenate(
            [jnp.where(slot == k, local, jnp.zeros_like(local)) for k in range(PACK)], axis=0
        )
        result = dot(spread, basis_ref[part].reshape(PACK * rank, width))
        out_ref[part] = (result.reshape(PACK, cases, width) + near_ref[part]).astype(BF16)


def shards(
    loads, basis, transfer, near_blocks, near_src, near_tgt, far_blocks, far_src, far_tgt,
    coarse_blocks, coarse_src, coarse_tgt
):
    leaves, cases, width = loads.shape
    rank = basis.shape[1]
    parents = leaves // 8
    tiles = (leaves + parents) // PACK
    count = lax.axis_size("branch")
    limit = 56 * 1024 * 1024
    far4 = jnp.tile(far_blocks, (1, 1, PACK))
    coarse4 = jnp.tile(coarse_blocks, (1, 1, PACK))
    mine = pl.pallas_call(
        upward,
        out_shape=jax.ShapeDtypeStruct((tiles, cases, PACK * rank), BF16),
        in_specs=[VMEM] * 3,
        out_specs=VMEM,
        compiler_params=pltpu.CompilerParams(vmem_limit_bytes=limit),
        name="upward",
    )(loads, basis, transfer)
    coef = lax.all_gather(mine, "branch", axis=0, tiled=True)
    left = lax.ppermute(loads, "branch", [(i, i + 1) for i in range(count - 1)])
    right = lax.ppermute(loads, "branch", [(i + 1, i) for i in range(count - 1)])
    chunk = 16
    entries = near_blocks.shape[0]
    near_field = pl.pallas_call(
        near,
        grid=(entries // chunk,),
        out_shape=jax.ShapeDtypeStruct((leaves, cases, width), F32),
        in_specs=[SMEM, SMEM]
        + [pl.BlockSpec((leaves, cases, width), lambda i: (0, 0, 0))] * 3
        + [pl.BlockSpec((chunk, width, width), lambda i: (i, 0, 0))],
        out_specs=pl.BlockSpec((leaves, cases, width), lambda i: (0, 0, 0)),
        scratch_shapes=[pltpu.VMEM((3 * leaves + 1, cases, width), BF16)],
        compiler_params=pltpu.CompilerParams(vmem_limit_bytes=limit),
        cost_estimate=pl.CostEstimate(
            flops=2 * entries * cases * width * width, bytes_accessed=12 * 2**20, transcendentals=0
        ),
        name="near",
    )(near_src, near_tgt, left, loads, right, near_blocks)
    return pl.pallas_call(
        downward,
        out_shape=jax.ShapeDtypeStruct((leaves, cases, width), BF16),
        in_specs=[SMEM] * 4 + [VMEM] * 6,
        out_specs=VMEM,
        scratch_shapes=[
            pltpu.VMEM((leaves // PACK, cases, PACK * rank), F32),
            pltpu.VMEM((parents, cases, PACK * rank), F32),
        ],
        compiler_params=pltpu.CompilerParams(vmem_limit_bytes=limit),
        name="downward",
    )(far_src, far_tgt, coarse_src, coarse_tgt, coef, far4, coarse4, transfer, basis, near_field)


def solution(mesh):
    spread = P(("rve", "branch"))
    return jax.shard_map(
        shards, mesh=mesh, in_specs=(spread,) * 12, out_specs=spread, check_vma=False
    )
```

time: 124 us -> 83 us (0.67)
  blocking collectives: 32.3 us -> 0 us
  waiting for transfers between devices: 0.02 us -> 31.1 us
  matrix products: 29.4 us -> 0 us
  local copies, waits for them, and re-layouts: 36.3 us -> 8.85 us
  Pallas kernels: 0 us -> 24.7 us
  other arithmetic: 5.39 us -> 0 us
    all_gather x1 -> x0, blocking collectives: 32.3 us -> none  [shards(): lax.all_gather(parent_flat, 'branch', axis=0, tiled=True)]
    all_gather x1, waiting for transfers between devices: 0.01 us -> 31 us  [shards(): coef = lax.all_gather(mine, 'branch', axis=0, tiled=True)]
    dot_general x9 -> x0, matrix products: 29.4 us -> none  [the longest x3 11.3 us: scatter_rows(): jnp.dot(selector, flat_terms, precision=lax.Precision.HIGHEST, preferred_...]
    pallas_call x0 -> x3, Pallas kernels: none -> 24.7 us  [the longest x1 12.3 us: shards(): pl.pallas_call(downward, out_shape=jax.ShapeDtypeStruct((leaves, cases, w...]
    gather x5 -> x0, local copies, waits for them, and re-layouts: 7.89 us -> none  [the longest x2 4.42 us: shards(): jnp.take(every_leaf, jnp.clip(far_src, 0, every_leaf.shape[0] - 1), axis=0)]
    another operation x0 -> x4, local copies, waits for them, and re-layouts: none -> 6.24 us  [the longest x2 4.44 us: shards(): far4 = jnp.tile(far_blocks, (1, 1, PACK))]
    mul x2 -> x0, local copies, waits for them, and re-layouts: 5.74 us -> none  [the longest x1 4.34 us: shards(): far_terms = far_terms * far_live.astype(jnp.float32)[:, None, None]]
    select_n x2 -> x0, local copies, waits for them, and re-layouts: 5.35 us -> none  [the longest x1 4.57 us: shards(): jnp.take(every_leaf, jnp.clip(far_src, 0, every_leaf.shape[0] - 1), axis=0)]
  transfers between devices with their start and end apart: 3 -> 3, of which waited for: 0 -> 1; matrix products, arithmetic and copies ran while one was open for 33% -> 8% of each run, Pallas kernels for 0% -> 11%
where the time goes in v1:
time: 83 us; the launch traced here: 82.7 us
  waiting for transfers between devices  31.1 us (37%)
  Pallas kernels  24.7 us (30%)
  between operations  13.4 us (16%)
  local copies, waits for them, and re-layouts  8.85 us (11%)
  starting transfers between devices  4.62 us (6%)
    all_gather x1, waiting for transfers between devices, shards(): coef = lax.all_gather(mine, 'branch', axis=0, tiled=True)  31 us
    pallas_call x1, Pallas kernels, shards(): pl.pallas_call(downward, out_shape=jax.ShapeDtypeStruct((leaves, cases, w...  12.3 us
    pallas_call x1, Pallas kernels, shards(): pl.pallas_call(near, grid=(entries // chunk,), out_shape=jax.ShapeDtypeSt...  8.83 us
    another operation x2, local copies, waits for them, and re-layouts, shards(): far4 = jnp.tile(far_blocks, (1, 1, PACK))  4.44 us
    pallas_call x1, Pallas kernels, shards(): pl.pallas_call(upward, out_shape=jax.ShapeDtypeStruct((tiles, cases, PACK...  3.61 us
    ppermute x1, starting transfers between devices, shards(): left = lax.ppermute(loads, 'branch', [(i, i + 1) for i in range(count - 1)])  3.34 us
    unnamed x5, local copies, waits for them, and re-layouts  2.62 us
    another operation x2, local copies, waits for them, and re-layouts, shards(): coarse4 = jnp.tile(coarse_blocks, (1, 1, PACK))  1.79 us
  transfers between devices with their start and end apart: 3, of which 1 were waited for; matrix products, arithmetic and copies ran while one was open for 8% of the time, Pallas kernels for 11%

profile of v1, /device:TPU:0, one launch (start us, length us, event | category | flops | bytes accessed | tf_op | source)
XLA Modules:
  0.0 82.7 jit_solution(4270469319976649853)
XLA Ops:
  6.5 0.0 copy-start
  6.5 0.0 all-gather.2.cloned.1.call-start
  6.5 2.6 %copy.21.transfer_ref = bf16[64,32,32]{2,1,0:T(8,128)(2,1)} copy(bf16[64,32,32]{0,2,1:T(8,128)(2,1)} %param.14) | data formatting | bytes 262144 | tf_op args[2]
  9.1 3.6 %upward.1 = bf16[18,32,128]{2,1,0:T(8,128)(2,1)} custom-call(bf16[64,32,192]{2,1,0:T(8,128)(2,1)} %own_ref.1, bf16[64,32,192]{2,1,0:T(8,128)(2,1)} %basis_ref.3, bf16[64,32,32]{2,1,0:T(8,128)(2,1)} %copy.21.transfer_ref), custom_call_target="tpu_custom_call" | custom-call | tf_op jit(solution)/shard_map/upward/pallas_call | solution.py:149
  12.8 0.0 all-gather.2.cloned.1.call-update
  12.8 0.0 copy-done
  12.8 3.3 %collective-permute-start = (bf16[64,32,192]{2,1,0:T(8,128)(2,1)S(1)}, bf16[64,32,192]{2,1,0:T(8,128)(2,1)}, u32[]{:S(2)}, u32[]{:S(2)}) collective-permute-start(bf16[64,32,192]{2,1,0:T(8,128)(2,1)S(1)} %copy-done), channel_id=1, source_target_pairs={{0,1},{1,2},{2,3},{3,4},{4,5},{5,6},{6,7},{7,8},{8,9},{9,10},{10,1... | collective-permute-start | bytes 2359304 | tf_op jit(solution)/shard_map/ppermute | solution.py:158
  16.1 1.3 %collective-permute-start.1 = (bf16[64,32,192]{2,1,0:T(8,128)(2,1)S(1)}, bf16[64,32,192]{2,1,0:T(8,128)(2,1)}, u32[]{:S(2)}, u32[]{:S(2)}) collective-permute-start(bf16[64,32,192]{2,1,0:T(8,128)(2,1)S(1)} %copy-done), channel_id=1, source_target_pairs={{1,0},{2,1},{3,2},{4,3},{5,4},{6,5},{7,6},{8,7},{9,8},{10,9},{11,1... | collective-permute-start | bytes 2359304 | tf_op jit(solution)/shard_map/ppermute | solution.py:159
  17.4 1.3 %tile.8 = bf16[256,32,4,32]{0,3,2,1:T(8,128)(2,1)S(1)} broadcast(bf16[256,32,32]{0,2,1:T(8,128)(2,1)} %param.18), dimensions={0,1,3} | broadcast | bytes 2621440 | tf_op jit(solution)/shard_map/tile | solution.py:147
  18.7 0.0 copy-start.1
  18.7 3.1 %copy.22.far_ref = bf16[256,32,128]{2,1,0:T(8,128)(2,1)} copy(bf16[256,32,128]{0,2,1:T(8,128)(2,1)S(1)} %bitcast.2) | data formatting | bytes 4194304 | tf_op jit(solution)/shard_map/tile | solution.py:147
  21.9 0.0 copy-done.1
  21.9 0.2 tile.20
  22.1 1.6 %copy.23.coarse_ref = bf16[64,32,128]{2,1,0:T(8,128)(2,1)} copy(bf16[64,32,128]{0,2,1:T(8,128)(2,1)S(1)} %bitcast.3) | data formatting | bytes 1048576 | tf_op jit(solution)/shard_map/tile | solution.py:148
  23.7 0.0 collective-permute-done.left_ref
  23.7 0.0 collective-permute-done.1.right_ref
  23.7 8.8 %near.1.near_ref = f32[64,32,192]{2,1,0:T(8,128)} custom-call(s32[96]{0:T(128)} %src_ref.1, s32[96]{0:T(128)} %tgt_ref.1, bf16[64,32,192]{2,1,0:T(8,128)(2,1)} %collective-permute-done.left_ref, bf16[64,32,192]{2,1,0:T(8,128)(2,1)} %own_ref.1, bf16[64,32,192]{2,1,0:T(8,128)(2,1)} %collective-permute-done.1.right_ref, bf16[96,192,192]{2,1,0:T(8,128)(2,1)} %blocks_ref.1), custom_call_target="tpu_custom_call" | custom-call | flops 226492416 | bytes 12582912 | tf_op jit(solution)/shard_map/near/pallas_call | solution.py:162
  32.5 31.0 %all-gather.2.cloned.1.call-done.coef_ref = bf16[288,32,128]{2,1,0:T(8,128)(2,1)} async-done(((bf16[18,32,128]{2,1,0:T(8,128)(2,1)}), bf16[288,32,128]{2,1,0:T(8,128)(2,1)}) %all-gather.2.cloned.1.call-update) | async-done | bytes 2359312 | tf_op jit(solution)/shard_map/all_gather | solution.py:157
  63.6 12.3 %downward.1 = bf16[64,32,192]{2,1,0:T(8,128)(2,1)} custom-call(s32[256]{0:T(256)} %fsrc_ref.1, s32[256]{0:T(256)} %ftgt_ref.1, s32[64]{0:T(128)} %csrc_ref.1, s32[64]{0:T(128)} %ctgt_ref.1, bf16[288,32,128]{2,1,0:T(8,128)(2,1)} %all-gather.2.cloned.1.call-done.coef_ref, bf16[256,32,128]{2,1,0:T(8,128)(2,1)} %copy.22.far_ref, ...), custom_call_target="tpu_custom_call" | custom-call | tf_op jit(solution)/shard_map/downward/pallas_call | solution.py:177
Async XLA Ops:
  6.5 6.2 %copy-start = (bf16[64,32,192]{2,1,0:T(8,128)(2,1)S(1)}, bf16[64,32,192]{2,1,0:T(8,128)(2,1)}, u32[]{:S(2)}) copy-start(bf16[64,32,192]{2,1,0:T(8,128)(2,1)} %own_ref.1) | copy-start | bytes 2359300
  6.5 57.0 %all-gather.2.cloned.1.call-start = ((), (), s32[]{:S(2)}) async-start(), calls=%async_computation | async-start | bytes 2506752 | tf_op jit(solution)/shard_map/all_gather | solution.py:157
  12.8 10.9 %collective-permute-start = (bf16[64,32,192]{2,1,0:T(8,128)(2,1)S(1)}, bf16[64,32,192]{2,1,0:T(8,128)(2,1)}, u32[]{:S(2)}, u32[]{:S(2)}) collective-permute-start(bf16[64,32,192]{2,1,0:T(8,128)(2,1)S(1)} %copy-done), channel_id=1, source_target_pairs={{0,1},{1,2},{2,3},{3,4},{4,5},{5,6},{6,7},{7,8},{8,9},{9,10},{10,1... | collective-permute-start | bytes 2359304 | tf_op jit(solution)/shard_map/ppermute | solution.py:158
  16.1 7.6 %collective-permute-start.1 = (bf16[64,32,192]{2,1,0:T(8,128)(2,1)S(1)}, bf16[64,32,192]{2,1,0:T(8,128)(2,1)}, u32[]{:S(2)}, u32[]{:S(2)}) collective-permute-start(bf16[64,32,192]{2,1,0:T(8,128)(2,1)S(1)} %copy-done), channel_id=1, source_target_pairs={{1,0},{2,1},{3,2},{4,3},{5,4},{6,5},{7,6},{8,7},{9,8},{10,9},{11,1... | collective-permute-start | bytes 2359304 | tf_op jit(solution)/shard_map/ppermute | solution.py:159
  18.7 3.2 %copy-start.1 = (bf16[64,32,32]{0,2,1:T(8,128)(2,1)S(1)}, bf16[64,32,32]{0,2,1:T(8,128)(2,1)}, u32[]{:S(2)}) copy-start(bf16[64,32,32]{0,2,1:T(8,128)(2,1)} %param.21) | copy-start | bytes 393220
Sparse Core Ops, SparseCore 0:
  12.9 50.6 all-gather.1

commit v2 on v1

--- a/solution.py
+++ b/solution.py
@@ -1,3 +1,5 @@
+import functools
+
 import jax
 import jax.numpy as jnp
 from jax import lax
@@ -7,6 +9,7 @@
 
 F32, BF16 = jnp.float32, jnp.bfloat16
 VMEM = pl.BlockSpec(memory_space=pltpu.VMEM)
+ANY = pl.BlockSpec(memory_space=pl.ANY)
 SMEM = pl.BlockSpec(memory_space=pltpu.SMEM)
 PACK = 4
 NT = (((1,), (1,)), ((), ()))
@@ -54,7 +57,80 @@
         out_ref[groups + h] = jnp.concatenate(parents[PACK * h : PACK * h + PACK], axis=1).astype(BF16)
 
 
-def near(src_ref, tgt_ref, left_ref, own_ref, right_ref, blocks_ref, out_ref, wide):
+def exchange(
+    n, loads_ref, basis_ref, transfer_ref, coef, mine, ring_send, ring_recv, pair_send, pair_recv, own_sem
+):
+    me = lax.axis_index("branch")
+    chips = n // 2
+    half = chips // 2
+    core = lax.rem(me, 2)
+    chip = lax.div(me, 2)
+    odd = lax.rem(chip, 2)
+    low = lax.div(chip, 2)
+    place = low + odd * (chips - 1 - 2 * low)
+
+    def at(position, core):
+        position = lax.rem(position + chips, chips)
+        far_side = lax.div(position, half)
+        return 2 * (2 * position + far_side * (2 * chips - 4 * position - 1)) + core
+
+    after, before = at(place + 1, core), at(place - 1, core)
+    partner = me + 1 - 2 * core
+    barrier = pltpu.get_barrier_semaphore()
+    for other in (after, before, partner):
+        pl.semaphore_signal(barrier, inc=1, device_id={"branch": other})
+    pl.semaphore_wait(barrier, 3)
+
+    upward(loads_ref, basis_ref, transfer_ref, mine)
+    own = pltpu.make_async_copy(mine, coef.at[me], own_sem)
+    own.start()
+
+    share = mine.shape[0] // 2
+    parts = [pl.ds(0, share), pl.ds(share, mine.shape[0] - share)]
+
+    def ring(way, h, step):
+        position = place - step if way == 0 else place + step
+        block = coef.at[at(position, core), parts[h]]
+        return pltpu.make_async_remote_copy(
+            src_ref=mine.at[parts[h]] if step == 0 else block, dst_ref=block,
+            send_sem=ring_send.at[way, h, step], recv_sem=ring_recv.at[way, h, step],
+            device_id={"branch": after if way == 0 else before},
+        )
+
+    def pair(k, src, dst):
+        return pltpu.make_async_remote_copy(
+            src_ref=src, dst_ref=dst, send_sem=pair_send.at[k], recv_sem=pair_recv.at[k],
+            device_id={"branch": partner},
+        )
+
+    copies = {
+        (way, h, step): ring(way, h, step)
+        for step in range(half)
+        for h in range(2)
+        for way in range(2)
+        if step < half - (way != h)
+    }
+    for key, copy in copies.items():
+        if key[2] == 0:
+            copy.start()
+    paired = [pair(0, mine, coef.at[me])]
+    paired[0].start()
+    for (way, h, step), copy in copies.items():
+        copy.wait_recv()
+        if (way, h, step + 1) in copies:
+            copies[way, h, step + 1].start()
+        position = place - 1 - step if way == 0 else place + 1 + step
+        block = coef.at[at(position, core), parts[h]]
+        paired.append(pair(1 + (2 * step + way) * 2 + h, block, block))
+        paired[-1].start()
+    for copy in paired:
+        copy.wait()
+    for copy in copies.values():
+        copy.wait_send()
+    own.wait()
+
+
+def near(src_ref, tgt_ref, left_ref, own_ref, right_ref, far_ref, blocks_ref, out_ref, wide, total):
     step = pl.program_id(0)
     leaves = own_ref.shape[0]
     base = lax.axis_index("branch") * leaves
@@ -66,7 +142,7 @@
         wide[pl.ds(leaves, leaves)] = own_ref[...]
         wide[pl.ds(2 * leaves, leaves)] = right_ref[...]
         wide[3 * leaves] = jnp.zeros(wide.shape[1:], BF16)
-        out_ref[...] = jnp.zeros_like(out_ref)
+        total[...] = far_ref[...]
 
     terms = []
     for i in range(chunk):
@@ -75,12 +151,16 @@
         terms.append(dot(wide[row], blocks_ref[i]))
     for i in range(chunk):
         t = jnp.clip(tgt_ref[step * chunk + i] - base, 0, leaves - 1)
-        out_ref[t] += terms[i]
+        total[t] += terms[i]
+
+    @pl.when(step == pl.num_programs(0) - 1)
+    def _():
+        out_ref[...] = total[...].astype(BF16)
 
 
 def downward(
     fsrc_ref, ftgt_ref, csrc_ref, ctgt_ref, coef_ref, far_ref, coarse_ref, transfer_ref, basis_ref,
-    near_ref, out_ref, facc, cacc
+    out_ref, facc, cacc
 ):
     leaves, rank, width = basis_ref.shape
     cases = out_ref.shape[1]
@@ -131,7 +211,7 @@
             [jnp.where(slot == k, local, jnp.zeros_like(local)) for k in range(PACK)], axis=0
         )
         result = dot(spread, basis_ref[part].reshape(PACK * rank, width))
-        out_ref[part] = (result.reshape(PACK, cases, width) + near_ref[part]).astype(BF16)
+        out_ref[part] = result.reshape(PACK, cases, width)
 
 
 def shards(
@@ -146,38 +226,36 @@
     limit = 56 * 1024 * 1024
     far4 = jnp.tile(far_blocks, (1, 1, PACK))
     coarse4 = jnp.tile(coarse_blocks, (1, 1, PACK))
-    mine = pl.pallas_call(
-        upward,
-        out_shape=jax.ShapeDtypeStruct((tiles, cases, PACK * rank), BF16),
-        in_specs=[VMEM] * 3,
-        out_specs=VMEM,
-        compiler_params=pltpu.CompilerParams(vmem_limit_bytes=limit),
-        name="upward",
-    )(loads, basis, transfer)
-    coef = lax.all_gather(mine, "branch", axis=0, tiled=True)
+    half = count // 4
     left = lax.ppermute(loads, "branch", [(i, i + 1) for i in range(count - 1)])
     right = lax.ppermute(loads, "branch", [(i + 1, i) for i in range(count - 1)])
+    (coef,) = pl.pallas_call(
+        functools.partial(exchange, count),
+        out_shape=(
+            jax.ShapeDtypeStruct((count, tiles, cases, PACK * rank), BF16),
+        ),
+        in_specs=[VMEM] * 3,
+        out_specs=(ANY,),
+        scratch_shapes=[
+            pltpu.VMEM((tiles, cases, PACK * rank), BF16),
+            pltpu.SemaphoreType.DMA((2, 2, half)),
+            pltpu.SemaphoreType.DMA((2, 2, half)),
+            pltpu.SemaphoreType.DMA((1 + 4 * half,)),
+            pltpu.SemaphoreType.DMA((1 + 4 * half,)),
+            pltpu.SemaphoreType.DMA,
+        ],
+        compiler_params=pltpu.CompilerParams(
+            collective_id=0, has_side_effects=True, vmem_limit_bytes=limit
+        ),
+        name="exchange",
+    )(loads, basis, transfer)
+    coef = coef.reshape(count * tiles, cases, PACK * rank)
     chunk = 16
     entries = near_blocks.shape[0]
-    near_field = pl.pallas_call(
-        near,
-        grid=(entries // chunk,),
+    far_field = pl.pallas_call(
+        downward,
         out_shape=jax.ShapeDtypeStruct((leaves, cases, width), F32),
-        in_specs=[SMEM, SMEM]
-        + [pl.BlockSpec((leaves, cases, width), lambda i: (0, 0, 0))] * 3
-        + [pl.BlockSpec((chunk, width, width), lambda i: (i, 0, 0))],
-        out_specs=pl.BlockSpec((leaves, cases, width), lambda i: (0, 0, 0)),
-        scratch_shapes=[pltpu.VMEM((3 * leaves + 1, cases, width), BF16)],
-        compiler_params=pltpu.CompilerParams(vmem_limit_bytes=limit),
-        cost_estimate=pl.CostEstimate(
-            flops=2 * entries * cases * width * width, bytes_accessed=12 * 2**20, transcendentals=0
-        ),
-        name="near",
-    )(near_src, near_tgt, left, loads, right, near_blocks)
-    return pl.pallas_call(
-        downward,
-        out_shape=jax.ShapeDtypeStruct((leaves, cases, width), BF16),
-        in_specs=[SMEM] * 4 + [VMEM] * 6,
+        in_specs=[SMEM] * 4 + [VMEM] * 5,
         out_specs=VMEM,
         scratch_shapes=[
             pltpu.VMEM((leaves // PACK, cases, PACK * rank), F32),
@@ -185,7 +263,25 @@
         ],
         compiler_params=pltpu.CompilerParams(vmem_limit_bytes=limit),
         name="downward",
-    )(far_src, far_tgt, coarse_src, coarse_tgt, coef, far4, coarse4, transfer, basis, near_field)
+    )(far_src, far_tgt, coarse_src, coarse_tgt, coef, far4, coarse4, transfer, basis)
+    return pl.pallas_call(
+        near,
+        grid=(entries // chunk,),
+        out_shape=jax.ShapeDtypeStruct((leaves, cases, width), BF16),
+        in_specs=[SMEM, SMEM]
+        + [pl.BlockSpec((leaves, cases, width), lambda i: (0, 0, 0))] * 4
+        + [pl.BlockSpec((chunk, width, width), lambda i: (i, 0, 0))],
+        out_specs=pl.BlockSpec((leaves, cases, width), lambda i: (0, 0, 0)),
+        scratch_shapes=[
+            pltpu.VMEM((3 * leaves + 1, cases, width), BF16),
+            pltpu.VMEM((leaves, cases, width), F32),
+        ],
+        compiler_params=pltpu.CompilerParams(vmem_limit_bytes=limit),
+        cost_estimate=pl.CostEstimate(
+            flops=2 * entries * cases * width * width, bytes_accessed=12 * 2**20, transcendentals=0
+        ),
+        name="near",
+    )(near_src, near_tgt, left, loads, right, far_field, near_blocks)
 
 
 def solution(mesh):

time: 83 us -> 74.1 us (0.89)
  Pallas kernels: 24.7 us -> 60.4 us
  waiting for transfers between devices: 31.1 us -> 0.01 us
  between operations: 13.4 us -> 0.06 us
  starting transfers between devices: 4.62 us -> 3.71 us
    pallas_call x1, Pallas kernels: 3.61 us -> 39.2 us  [shards(): pl.pallas_call(functools.partial(exchange, count), out_shape=(jax.ShapeDt...]
    all_gather x1 -> x0, waiting for transfers between devices: 31 us -> none  [shards(): coef = lax.all_gather(mine, 'branch', axis=0, tiled=True)]
    ppermute x1, starting transfers between devices: 3.34 us -> 2.41 us  [shards(): left = lax.ppermute(loads, 'branch', [(i, i + 1) for i in range(count - 1)])]
  transfers between devices with their start and end apart: 3 -> 2, of which waited for: 1 -> 0; matrix products, arithmetic and copies ran while one was open for 8% -> 12% of each run, Pallas kernels for 11% -> 69%
where the time goes in v2:
time: 74.1 us; the launch traced here: 73.8 us
  Pallas kernels  60.4 us (82%)
  local copies, waits for them, and re-layouts  9.63 us (13%)
  starting transfers between devices  3.71 us (5%)
    pallas_call x1, Pallas kernels, shards(): pl.pallas_call(functools.partial(exchange, count), out_shape=(jax.ShapeDt...  39.2 us
    pallas_call x1, Pallas kernels, shards(): pl.pallas_call(downward, out_shape=jax.ShapeDtypeStruct((leaves, cases, w...  11.9 us
    pallas_call x1, Pallas kernels, shards(): pl.pallas_call(near, grid=(entries // chunk,), out_shape=jax.ShapeDtypeSt...  9.24 us
    another operation x2, local copies, waits for them, and re-layouts, shards(): far4 = jnp.tile(far_blocks, (1, 1, PACK))  4.42 us
    unnamed x5, local copies, waits for them, and re-layouts  3.42 us
    ppermute x1, starting transfers between devices, shards(): left = lax.ppermute(loads, 'branch', [(i, i + 1) for i in range(count - 1)])  2.41 us
    another operation x2, local copies, waits for them, and re-layouts, shards(): coarse4 = jnp.tile(coarse_blocks, (1, 1, PACK))  1.79 us
  transfers between devices with their start and end apart: 2, of which 0 were waited for; matrix products, arithmetic and copies ran while one was open for 12% of the time, Pallas kernels for 69%

profile of v2, /device:TPU:0, one launch (start us, length us, event | category | flops | bytes accessed | tf_op | source)
XLA Modules:
  0.0 73.8 jit_solution(4104891576412675765)
XLA Ops:
  0.0 2.4 %collective-permute-start = (bf16[64,32,192]{2,1,0:T(8,128)(2,1)}, bf16[64,32,192]{2,1,0:T(8,128)(2,1)S(1)}, u32[]{:S(2)}, u32[]{:S(2)}) collective-permute-start(bf16[64,32,192]{2,1,0:T(8,128)(2,1)} %own_ref.1), channel_id=1, source_target_pairs={{0,1},{1,2},{2,3},{3,4},{4,5},{5,6},{6,7},{7,8},{8,9},{9,10},{10,1... | collective-permute-start | bytes 2359304 | tf_op jit(solution)/shard_map/ppermute | solution.py:230
  2.4 1.3 %collective-permute-start.1 = (bf16[64,32,192]{2,1,0:T(8,128)(2,1)}, bf16[64,32,192]{2,1,0:T(8,128)(2,1)}, u32[]{:S(2)}, u32[]{:S(2)}) collective-permute-start(bf16[64,32,192]{2,1,0:T(8,128)(2,1)} %own_ref.1), channel_id=1, source_target_pairs={{1,0},{2,1},{3,2},{4,3},{5,4},{6,5},{7,6},{8,7},{9,8},{10,9},{11,1... | collective-permute-start | bytes 2359304 | tf_op jit(solution)/shard_map/ppermute | solution.py:231
  3.7 2.5 %copy.17.transfer_ref = bf16[64,32,32]{2,1,0:T(8,128)(2,1)} copy(bf16[64,32,32]{0,2,1:T(8,128)(2,1)} %param.14) | data formatting | bytes 262144 | tf_op args[2]
  6.2 1.3 %tile.8 = bf16[256,32,4,32]{0,3,2,1:T(8,128)(2,1)S(1)} broadcast(bf16[256,32,32]{0,2,1:T(8,128)(2,1)} %param.18), dimensions={0,1,3} | broadcast | bytes 2621440 | tf_op jit(solution)/shard_map/tile | solution.py:227
  7.5 0.0 copy-start.1
  7.5 3.1 %copy.18.far_ref = bf16[256,32,128]{2,1,0:T(8,128)(2,1)} copy(bf16[256,32,128]{0,2,1:T(8,128)(2,1)S(1)} %bitcast.4) | data formatting | bytes 4194304 | tf_op jit(solution)/shard_map/tile | solution.py:227
  10.6 0.0 copy-done.1
  10.6 0.2 tile.20
  10.8 1.6 %copy.19.coarse_ref = bf16[64,32,128]{2,1,0:T(8,128)(2,1)} copy(bf16[64,32,128]{0,2,1:T(8,128)(2,1)S(1)} %bitcast.5) | data formatting | bytes 1048576 | tf_op jit(solution)/shard_map/tile | solution.py:228
  12.4 39.2 %exchange.1 = bf16[16,18,32,128]{3,2,1,0:T(8,128)(2,1)} custom-call(bf16[64,32,192]{2,1,0:T(8,128)(2,1)} %own_ref.1, bf16[64,32,192]{2,1,0:T(8,128)(2,1)} %basis_ref.3, bf16[64,32,32]{2,1,0:T(8,128)(2,1)} %copy.17.transfer_ref), custom_call_target="tpu_custom_call" | custom-call | tf_op jit(solution)/shard_map/exchange/pallas_call | solution.py:232
  51.7 11.9 %downward.1.far_ref = f32[64,32,192]{2,1,0:T(8,128)} custom-call(s32[256]{0:T(256)} %fsrc_ref.1, s32[256]{0:T(256)} %ftgt_ref.1, s32[64]{0:T(128)} %csrc_ref.1, s32[64]{0:T(128)} %ctgt_ref.1, bf16[288,32,128]{2,1,0:T(8,128)(2,1)} %bitcast.3, bf16[256,32,128]{2,1,0:T(8,128)(2,1)} %copy.18.far_ref, bf16[64,32,128]{2,1,0:T(8,128)(2,1)} %copy.19.coarse_ref, ...), custom_call_target="tpu_custom_call" | custom-call | tf_op jit(solution)/shard_map/downward/pallas_call | solution.py:255
  63.6 0.0 collective-permute-done.left_ref
  63.6 0.0 copy-start
  63.6 0.0 collective-permute-done.1.right_ref
  63.6 1.0 %copy-done = bf16[64,32,192]{2,1,0:T(8,128)(2,1)} copy-done((bf16[64,32,192]{2,1,0:T(8,128)(2,1)}, bf16[64,32,192]{2,1,0:T(8,128)(2,1)S(1)}, u32[]{:S(2)}) %copy-start) | copy-done | bytes 786456
  64.6 9.2 %near.1 = bf16[64,32,192]{2,1,0:T(8,128)(2,1)} custom-call(s32[96]{0:T(128)} %src_ref.1, s32[96]{0:T(128)} %tgt_ref.1, bf16[64,32,192]{2,1,0:T(8,128)(2,1)} %copy-done, bf16[64,32,192]{2,1,0:T(8,128)(2,1)} %own_ref.1, bf16[64,32,192]{2,1,0:T(8,128)(2,1)} %collective-permute-done.1.right_ref, f32[64,32,192]{2,1,0:T(8,128)} %downward.1.far_ref, ...), custom_call_target="tpu_custom_call" | custom-call | flops 226492416 | bytes 12582912 | tf_op jit(solution)/shard_map/near/pallas_call | solution.py:267
Async XLA Ops:
  0.0 63.6 %collective-permute-start = (bf16[64,32,192]{2,1,0:T(8,128)(2,1)}, bf16[64,32,192]{2,1,0:T(8,128)(2,1)S(1)}, u32[]{:S(2)}, u32[]{:S(2)}) collective-permute-start(bf16[64,32,192]{2,1,0:T(8,128)(2,1)} %own_ref.1), channel_id=1, source_target_pairs={{0,1},{1,2},{2,3},{3,4},{4,5},{5,6},{6,7},{7,8},{8,9},{9,10},{10,1... | collective-permute-start | bytes 2359304 | tf_op jit(solution)/shard_map/ppermute | solution.py:230
  2.4 61.2 %collective-permute-start.1 = (bf16[64,32,192]{2,1,0:T(8,128)(2,1)}, bf16[64,32,192]{2,1,0:T(8,128)(2,1)}, u32[]{:S(2)}, u32[]{:S(2)}) collective-permute-start(bf16[64,32,192]{2,1,0:T(8,128)(2,1)} %own_ref.1), channel_id=1, source_target_pairs={{1,0},{2,1},{3,2},{4,3},{5,4},{6,5},{7,6},{8,7},{9,8},{10,9},{11,1... | collective-permute-start | bytes 2359304 | tf_op jit(solution)/shard_map/ppermute | solution.py:231
  7.5 3.1 %copy-start.1 = (bf16[64,32,32]{0,2,1:T(8,128)(2,1)S(1)}, bf16[64,32,32]{0,2,1:T(8,128)(2,1)}, u32[]{:S(2)}) copy-start(bf16[64,32,32]{0,2,1:T(8,128)(2,1)} %param.21) | copy-start | bytes 393220
  63.6 1.0 %copy-start = (bf16[64,32,192]{2,1,0:T(8,128)(2,1)}, bf16[64,32,192]{2,1,0:T(8,128)(2,1)S(1)}, u32[]{:S(2)}) copy-start(bf16[64,32,192]{2,1,0:T(8,128)(2,1)S(1)} %collective-permute-done.left_ref) | copy-start | bytes 2359300

commit v3 on v2

--- a/solution.py
+++ b/solution.py
@@ -144,14 +144,15 @@
         wide[3 * leaves] = jnp.zeros(wide.shape[1:], BF16)
         total[...] = far_ref[...]
 
-    terms = []
-    for i in range(chunk):
-        s = src_ref[step * chunk + i]
-        row = jnp.where(s < 0, 3 * leaves, jnp.clip(s - base + leaves, 0, 3 * leaves - 1))
-        terms.append(dot(wide[row], blocks_ref[i]))
-    for i in range(chunk):
-        t = jnp.clip(tgt_ref[step * chunk + i] - base, 0, leaves - 1)
-        total[t] += terms[i]
+    for first in range(0, chunk, 16):
+        terms = []
+        for i in range(first, first + 16):
+            s = src_ref[step * chunk + i]
+            row = jnp.where(s < 0, 3 * leaves, jnp.clip(s - base + leaves, 0, 3 * leaves - 1))
+            terms.append(dot(wide[row], blocks_ref[i]))
+        for i in range(first, first + 16):
+            t = jnp.clip(tgt_ref[step * chunk + i] - base, 0, leaves - 1)
+            total[t] += terms[i - first]
 
     @pl.when(step == pl.num_programs(0) - 1)
     def _():
@@ -183,7 +184,7 @@
         lhs = jnp.where(slot == k, lhs, jnp.zeros_like(lhs))
         return dot(lhs, jnp.concatenate([block_ref[j]] * PACK, axis=0))
 
-    unroll = 16
+    unroll = 64
 
     def far_step(i, carry):
         terms = [couple(fsrc_ref, far_ref, leaves, 0, i * unroll + u) for u in range(unroll)]
@@ -250,7 +251,7 @@
         name="exchange",
     )(loads, basis, transfer)
     coef = coef.reshape(count * tiles, cases, PACK * rank)
-    chunk = 16
+    chunk = 32
     entries = near_blocks.shape[0]
     far_field = pl.pallas_call(
         downward,

time: 74.1 us -> 71.3 us (0.962)
  Pallas kernels: 60.4 us -> 57.6 us
    pallas_call x1, Pallas kernels: 11.9 us -> 10.1 us  [shards(): pl.pallas_call(downward, out_shape=jax.ShapeDtypeStruct((leaves, cases, w...]
    pallas_call x1, Pallas kernels: 9.24 us -> 8.21 us  [shards(): pl.pallas_call(near, grid=(entries // chunk,), out_shape=jax.ShapeDtypeSt...]
  transfers between devices with their start and end apart: 2 -> 2, of which waited for: 0 -> 0; matrix products, arithmetic and copies ran while one was open for 12% -> 12% of each run, Pallas kernels for 69% -> 70%
where the time goes in v3:
time: 71.3 us; the launch traced here: 71 us
  Pallas kernels  57.6 us (81%)
  local copies, waits for them, and re-layouts  9.63 us (14%)
  starting transfers between devices  3.71 us (5%)
    pallas_call x1, Pallas kernels, shards(): pl.pallas_call(functools.partial(exchange, count), out_shape=(jax.ShapeDt...  39.2 us
    pallas_call x1, Pallas kernels, shards(): pl.pallas_call(downward, out_shape=jax.ShapeDtypeStruct((leaves, cases, w...  10.1 us
    pallas_call x1, Pallas kernels, shards(): pl.pallas_call(near, grid=(entries // chunk,), out_shape=jax.ShapeDtypeSt...  8.21 us
    another operation x2, local copies, waits for them, and re-layouts, shards(): far4 = jnp.tile(far_blocks, (1, 1, PACK))  4.42 us
    unnamed x5, local copies, waits for them, and re-layouts  3.42 us
    ppermute x1, starting transfers between devices, shards(): left = lax.ppermute(loads, 'branch', [(i, i + 1) for i in range(count - 1)])  2.41 us
    another operation x2, local copies, waits for them, and re-layouts, shards(): coarse4 = jnp.tile(coarse_blocks, (1, 1, PACK))  1.79 us
  transfers between devices with their start and end apart: 2, of which 0 were waited for; matrix products, arithmetic and copies ran while one was open for 12% of the time, Pallas kernels for 70%

profile of v3, /device:TPU:0, one launch (start us, length us, event | category | flops | bytes accessed | tf_op | source)
XLA Modules:
  0.0 71.0 jit_solution(11109351954284356895)
XLA Ops:
  0.0 2.4 %collective-permute-start = (bf16[64,32,192]{2,1,0:T(8,128)(2,1)}, bf16[64,32,192]{2,1,0:T(8,128)(2,1)S(1)}, u32[]{:S(2)}, u32[]{:S(2)}) collective-permute-start(bf16[64,32,192]{2,1,0:T(8,128)(2,1)} %own_ref.1), channel_id=1, source_target_pairs={{0,1},{1,2},{2,3},{3,4},{4,5},{5,6},{6,7},{7,8},{8,9},{9,10},{10,1... | collective-permute-start | bytes 2359304 | tf_op jit(solution)/shard_map/ppermute | solution.py:231
  2.4 1.3 %collective-permute-start.1 = (bf16[64,32,192]{2,1,0:T(8,128)(2,1)}, bf16[64,32,192]{2,1,0:T(8,128)(2,1)}, u32[]{:S(2)}, u32[]{:S(2)}) collective-permute-start(bf16[64,32,192]{2,1,0:T(8,128)(2,1)} %own_ref.1), channel_id=1, source_target_pairs={{1,0},{2,1},{3,2},{4,3},{5,4},{6,5},{7,6},{8,7},{9,8},{10,9},{11,1... | collective-permute-start | bytes 2359304 | tf_op jit(solution)/shard_map/ppermute | solution.py:232
  3.7 2.5 %copy.17.transfer_ref = bf16[64,32,32]{2,1,0:T(8,128)(2,1)} copy(bf16[64,32,32]{0,2,1:T(8,128)(2,1)} %param.14) | data formatting | bytes 262144 | tf_op args[2]
  6.2 1.3 %tile.8 = bf16[256,32,4,32]{0,3,2,1:T(8,128)(2,1)S(1)} broadcast(bf16[256,32,32]{0,2,1:T(8,128)(2,1)} %param.18), dimensions={0,1,3} | broadcast | bytes 2621440 | tf_op jit(solution)/shard_map/tile | solution.py:228
  7.5 0.0 copy-start.1
  7.5 3.1 %copy.18.far_ref = bf16[256,32,128]{2,1,0:T(8,128)(2,1)} copy(bf16[256,32,128]{0,2,1:T(8,128)(2,1)S(1)} %bitcast.4) | data formatting | bytes 4194304 | tf_op jit(solution)/shard_map/tile | solution.py:228
  10.6 0.0 copy-done.1
  10.6 0.2 tile.20
  10.8 1.6 %copy.19.coarse_ref = bf16[64,32,128]{2,1,0:T(8,128)(2,1)} copy(bf16[64,32,128]{0,2,1:T(8,128)(2,1)S(1)} %bitcast.5) | data formatting | bytes 1048576 | tf_op jit(solution)/shard_map/tile | solution.py:229
  12.4 39.2 %exchange.1 = bf16[16,18,32,128]{3,2,1,0:T(8,128)(2,1)} custom-call(bf16[64,32,192]{2,1,0:T(8,128)(2,1)} %own_ref.1, bf16[64,32,192]{2,1,0:T(8,128)(2,1)} %basis_ref.3, bf16[64,32,32]{2,1,0:T(8,128)(2,1)} %copy.17.transfer_ref), custom_call_target="tpu_custom_call" | custom-call | tf_op jit(solution)/shard_map/exchange/pallas_call | solution.py:233
  51.7 10.1 %downward.1.far_ref = f32[64,32,192]{2,1,0:T(8,128)} custom-call(s32[256]{0:T(256)} %fsrc_ref.1, s32[256]{0:T(256)} %ftgt_ref.1, s32[64]{0:T(128)} %csrc_ref.1, s32[64]{0:T(128)} %ctgt_ref.1, bf16[288,32,128]{2,1,0:T(8,128)(2,1)} %bitcast.3, bf16[256,32,128]{2,1,0:T(8,128)(2,1)} %copy.18.far_ref, bf16[64,32,128]{2,1,0:T(8,128)(2,1)} %copy.19.coarse_ref, ...), custom_call_target="tpu_custom_call" | custom-call | tf_op jit(solution)/shard_map/downward/pallas_call | solution.py:256
  61.8 0.0 collective-permute-done.left_ref
  61.8 0.0 copy-start
  61.8 0.0 collective-permute-done.1.right_ref
  61.8 1.0 %copy-done = bf16[64,32,192]{2,1,0:T(8,128)(2,1)} copy-done((bf16[64,32,192]{2,1,0:T(8,128)(2,1)}, bf16[64,32,192]{2,1,0:T(8,128)(2,1)S(1)}, u32[]{:S(2)}) %copy-start) | copy-done | bytes 786456
  62.8 8.2 %near.1 = bf16[64,32,192]{2,1,0:T(8,128)(2,1)} custom-call(s32[96]{0:T(128)} %src_ref.1, s32[96]{0:T(128)} %tgt_ref.1, bf16[64,32,192]{2,1,0:T(8,128)(2,1)} %copy-done, bf16[64,32,192]{2,1,0:T(8,128)(2,1)} %own_ref.1, bf16[64,32,192]{2,1,0:T(8,128)(2,1)} %collective-permute-done.1.right_ref, f32[64,32,192]{2,1,0:T(8,128)} %downward.1.far_ref, ...), custom_call_target="tpu_custom_call" | custom-call | flops 226492416 | bytes 12582912 | tf_op jit(solution)/shard_map/near/pallas_call | solution.py:268
Async XLA Ops:
  0.0 61.8 %collective-permute-start = (bf16[64,32,192]{2,1,0:T(8,128)(2,1)}, bf16[64,32,192]{2,1,0:T(8,128)(2,1)S(1)}, u32[]{:S(2)}, u32[]{:S(2)}) collective-permute-start(bf16[64,32,192]{2,1,0:T(8,128)(2,1)} %own_ref.1), channel_id=1, source_target_pairs={{0,1},{1,2},{2,3},{3,4},{4,5},{5,6},{6,7},{7,8},{8,9},{9,10},{10,1... | collective-permute-start | bytes 2359304 | tf_op jit(solution)/shard_map/ppermute | solution.py:231
  2.4 59.4 %collective-permute-start.1 = (bf16[64,32,192]{2,1,0:T(8,128)(2,1)}, bf16[64,32,192]{2,1,0:T(8,128)(2,1)}, u32[]{:S(2)}, u32[]{:S(2)}) collective-permute-start(bf16[64,32,192]{2,1,0:T(8,128)(2,1)} %own_ref.1), channel_id=1, source_target_pairs={{1,0},{2,1},{3,2},{4,3},{5,4},{6,5},{7,6},{8,7},{9,8},{10,9},{11,1... | collective-permute-start | bytes 2359304 | tf_op jit(solution)/shard_map/ppermute | solution.py:232
  7.5 3.1 %copy-start.1 = (bf16[64,32,32]{0,2,1:T(8,128)(2,1)S(1)}, bf16[64,32,32]{0,2,1:T(8,128)(2,1)}, u32[]{:S(2)}) copy-start(bf16[64,32,32]{0,2,1:T(8,128)(2,1)} %param.21) | copy-start | bytes 393220
  61.8 1.0 %copy-start = (bf16[64,32,192]{2,1,0:T(8,128)(2,1)}, bf16[64,32,192]{2,1,0:T(8,128)(2,1)S(1)}, u32[]{:S(2)}) copy-start(bf16[64,32,192]{2,1,0:T(8,128)(2,1)S(1)} %collective-permute-done.left_ref) | copy-start | bytes 2359300
